TPU v7x, 128 devices: a whole 4x4x4 slice. The times are simulated.
128 devices in a mesh: ctx: 16 (over y_lo, z, core), head: 8 (over y_hi, x).
Axes of the slice: x: 4, y: 4 (y_hi: 2, y_lo: 2; y = y_hi * 2 + y_lo), z: 4, core: 2. Of those that a mesh axis runs over, the one named last changes fastest.
Arguments:
- queries: bfloat16 [16384, 8192], P(('ctx', 'head')), may hold values from -128 to 128
- keys: bfloat16 [16384, 1024], P(('ctx', 'head')), may hold values from -8 to 8
- values: bfloat16 [16384, 1024], P(('ctx', 'head')), may hold values from -6 to 6
- doc_lengths: int32 [8], replicated, may hold values from 1 to 6144, 16384 in all
Outputs:
- attended: bfloat16 [16384, 8192], P(('ctx', 'head'))
Inputs may be any that keep to these rules, and one draw needn't show every extreme that they name: `doc_lengths`: each document has 1 to 6144 tokens, the longest exactly 6144; they sum to 16384.
All inputs are finite; a program needn't handle non-finite values.
Results may differ from a plain program's by a relative error of at most 0.005.
Values may be sent and summed in bfloat16 or wider, within the bound.
A program may use at most 128 MiB of HBM per device.

v0:
```python
import jax
import jax.numpy as jnp
from jax import lax
from jax.sharding import PartitionSpec as P

HEAD_DIM = 128
REACH = 6


def from_behind(block, axis, distance):
    devices = range(lax.axis_size(axis))
    route = [(i - distance, i) for i in devices if i - distance in devices]
    return lax.ppermute(block, axis, route)


def doc_starts(positions, doc_lengths):
    ends = jnp.cumsum(doc_lengths)
    return jnp.sum(jnp.where(ends[None, :] <= positions[:, None], doc_lengths[None, :], 0), axis=1)


def on_device(queries, keys, values, doc_lengths):
    gathered_q, gathered_k, gathered_v = (
        lax.all_to_all(queries, "head", split_axis=1, concat_axis=0, tiled=True),
        lax.all_to_all(keys, "head", split_axis=1, concat_axis=0, tiled=True),
        lax.all_to_all(values, "head", split_axis=1, concat_axis=0, tiled=True),
    )
    span = gathered_q.shape[0]
    kv_dev = gathered_k.shape[1] // HEAD_DIM
    q_dev = gathered_q.shape[1] // HEAD_DIM
    group = q_dev // kv_dev
    qblock = min(512, span)
    nblocks = span // qblock
    ctx_index = lax.axis_index("ctx")
    q_first = ctx_index * span
    q_pos = q_first + jnp.arange(span, dtype=jnp.int32)
    starts = doc_starts(q_pos, doc_lengths)
    lowest = jnp.min(starts)
    q_four = gathered_q.reshape(nblocks, qblock, kv_dev, group, HEAD_DIM)
    q_pos_blk = q_pos.reshape(nblocks, qblock)
    starts_blk = starts.reshape(nblocks, qblock)
    scale = HEAD_DIM ** (-0.5)

    def update(state, key_block, value_block, k_first):
        top_all, den_all, acc_all = state
        count = key_block.shape[0]
        k_three = key_block.reshape(count, kv_dev, HEAD_DIM)
        v_three = value_block.reshape(count, kv_dev, HEAD_DIM)
        k_pos = k_first + jnp.arange(count, dtype=jnp.int32)
        for index in range(nblocks):
            visible = (k_pos[None, :] >= starts_blk[index][:, None]) & (
                k_pos[None, :] <= q_pos_blk[index][:, None]
            )
            scores = (
                jnp.einsum(
                    "qkgd,wkd->kgqw", q_four[index], k_three, preferred_element_type=jnp.float32
                )
                * scale
            )
            masked = jnp.where(visible[None, None], scores, -1e30)
            old_top = top_all[index]
            new_top = jnp.maximum(old_top, jnp.max(masked, axis=-1))
            factor = jnp.exp(old_top - new_top)
            expo = jnp.where(visible[None, None], jnp.exp(masked - new_top[..., None]), 0.0)
            den_new = den_all[index] * factor + jnp.sum(expo, axis=-1)
            product = jnp.einsum(
                "kgqw,wkd->kgqd",
                expo.astype(jnp.bfloat16),
                v_three,
                preferred_element_type=jnp.float32,
            )
            acc_new = acc_all[index] * factor[..., None] + product
            top_all = top_all.at[index].set(new_top)
            den_all = den_all.at[index].set(den_new)
            acc_all = acc_all.at[index].set(acc_new)
        return (top_all, den_all, acc_all)

    def attend(state, key_block, value_block, k_first):
        count = key_block.shape[0]
        live = (k_first + count > lowest) & (k_first <= q_first + span - 1)
        return lax.cond(
            live, lambda st: update(st, key_block, value_block, k_first), lambda st: st, state
        )

    state = (
        jnp.full((nblocks, kv_dev, group, qblock), -1e30, jnp.float32),
        jnp.zeros((nblocks, kv_dev, group, qblock), jnp.float32),
        jnp.zeros((nblocks, kv_dev, group, qblock, HEAD_DIM), jnp.float32),
    )
    paired = jnp.stack((gathered_k, gathered_v))
    state = attend(state, gathered_k, gathered_v, q_first)
    moving = paired
    for step in range(1, REACH + 1):
        moving = from_behind(moving, "ctx", 1)
        state = attend(state, moving[0], moving[1], (ctx_index - step) * span)
    top_all, den_all, acc_all = state
    result = acc_all / den_all[..., None]
    result = (
        jnp.transpose(result, (0, 3, 1, 2, 4)).reshape(span, q_dev * HEAD_DIM).astype(jnp.bfloat16)
    )
    return lax.all_to_all(result, "head", split_axis=0, concat_axis=1, tiled=True)


def solution(mesh):
    placed = (P(("ctx", "head"), None), P(("ctx", "head"), None), P(("ctx", "head"), None), P())
    return jax.shard_map(
        on_device, mesh=mesh, in_specs=placed, out_specs=P(("ctx", "head"), None), check_vma=False
    )
```

profile of v0, /device:TPU:105, one launch (start us, length us, event | category | flops | bytes accessed | tf_op | source)
XLA Modules:
  0.0 356.4 jit_solution(6478936162480081717)
XLA Ops:
  8.5 6.8 %all-to-all-done.1 = bf16[128,8,128]{2,0,1:T(8,128)(2,1)S(1)} async-done(((bf16[128,8,128]{2,0,1:T(8,128)(2,1)}), bf16[128,8,128]{2,0,1:T(8,128)(2,1)S(1)}, u32[]{:S(2)}, u32[]{:S(2)}) %all-to-all-start.1) | async-done | bytes 262176 | tf_op jit(solution)/shard_map/all_to_all | solution.py:24
  15.3 10.1 %all_to_all.70 = bf16[128,8,128]{2,0,1:T(8,128)(2,1)S(1)} all-to-all(bf16[128,8,128]{2,0,1:T(8,128)(2,1)S(1)} %copy_bitcast_fusion.1), channel_id=1, replica_groups=mesh['ctx'=16,'head'=8] {'head'}, dimensions={1} | all-to-all | bytes 524288 | tf_op jit(solution)/shard_map/all_to_all | solution.py:25
  33.2 9.2 %collective-permute-done.1 = bf16[2,1024,128]{2,1,0:T(8,128)(2,1)S(1)} collective-permute-done((bf16[2,1024,128]{2,1,0:T(8,128)(2,1)S(1)}, bf16[2,1024,128]{2,1,0:T(8,128)(2,1)S(1)}, u32[]{:S(2)}, u32[]{:S(2)}) %collective-permute-start.1) | collective-permute-done | bytes 524320 | tf_op jit(solution)/shard_map/ppermute | solution.py:13
  54.3 9.5 %collective-permute-done.3 = bf16[2,1024,128]{2,1,0:T(8,128)(2,1)} collective-permute-done((bf16[2,1024,128]{2,1,0:T(8,128)(2,1)}, bf16[2,1024,128]{2,1,0:T(8,128)(2,1)}, u32[]{:S(2)}, u32[]{:S(2)}) %collective-permute-start.3) | collective-permute-done | bytes 524320 | tf_op jit(solution)/shard_map/ppermute | solution.py:13
  82.4 30.4 %conditional.7 = (f32[2,1,8,512]{3,2,1,0:T(8,128)S(1)}, f32[2,1,8,512]{3,2,1,0:T(8,128)S(1)}, f32[2,1,8,512,128]{4,3,2,1,0:T(8,128)}) conditional(s32[]{:T(128)} %convert_element_type.79, () %tuple.214, (s32[]{:T(128)}, s32[2,512]{1,0:T(2,128)S(1)}, s32[2,512]{1,0:T(2,128)S(1)}, bf16[2,512,1,8,128]{4,3,1,0,2:T(8,128)(2,1)S(1)}, ...), branch_computations={%region_3.4_spmd, %region_4.9_spmd} | conditional | flops 4409320448 | bytes 125337624 | solution.py:80
  112.8 32.1 %conditional.8 = ((f32[2,1,8,512]{3,2,1,0:T(8,128)S(1)}, f32[2,1,8,512]{3,2,1,0:T(8,128)S(1)}, f32[2,1,8,512,128]{4,3,2,1,0:T(8,128)})) conditional(s32[]{:T(128)} %convert_element_type.78, (f32[2,1,8,512]{3,2,1,0:T(8,128)S(1)}, f32[2,1,8,512]{3,2,1,0:T(8,128)S(1)}, f32[2,1,8,512,128]{4,3,2,1,0:T(8,128)}) %conditional.7, ...), branch_computations={%region_9.10_spmd, %region_10.15_spmd} | conditional | flops 4409295872 | bytes 126353464 | solution.py:80
  119.6 6.3 %bitcast_dynamic-update-slice_fusion = f32[2,1,8,512,128]{4,3,2,1,0:T(8,128)} fusion(f32[2,1,8,512,128]{4,3,2,1,0:T(8,128)} %get-tuple-element.666, f32[1,1,8,512,128]{4,3,2,1,0:T(8,128)S(1)} %slice.1294, f32[1024,512,8]{1,0,2:T(8,128)S(1)} %get-tuple-element.978, f32[8,512]{1,0:T(8,128)S(1)} %get-tuple-element.928, ...), kind=kOutput, calls=%fused_computation.67 | convolution fusion | flops 1095761920 | bytes 21790720 | tf_op jit(solution)/shard_map/cond/branch_1_fun/kgqw,wkd->kgqd/dot_general | solution.py:65
  133.5 7.3 %fusion.49 = f32[2,1,8,512,128]{4,3,2,1,0:T(8,128)} fusion(f32[2,1,8,512,128]{4,3,2,1,0:T(8,128)} %bitcast_dynamic-update-slice_fusion, f32[1024,512,8]{1,0,2:T(8,128)S(1)} %get-tuple-element.980, f32[8,512]{1,0:T(8,128)S(1)} %get-tuple-element.926, pred[512,1024]{0,1:T(8,128)(4,1)S(1)} %get-tuple-element.971, f32[8,512]{1,0:T(8,128)S(1)} %get-tuple-element.925, ...), kind=kOutput, calls=%fused_computation.66 | convolution fusion | flops 1095761920 | bytes 21790720 | tf_op jit(solution)/shard_map/cond/branch_1_fun/kgqw,wkd->kgqd/dot_general | solution.py:65
  144.8 32.1 %conditional.9 = ((f32[2,1,8,512]{3,2,1,0:T(8,128)S(1)}, f32[2,1,8,512]{3,2,1,0:T(8,128)S(1)}, f32[2,1,8,512,128]{4,3,2,1,0:T(8,128)})) conditional(s32[]{:T(128)} %convert_element_type.77, (f32[2,1,8,512]{3,2,1,0:T(8,128)S(1)}, f32[2,1,8,512]{3,2,1,0:T(8,128)S(1)}, f32[2,1,8,512,128]{4,3,2,1,0:T(8,128)}) %get-tuple-element.1109, ...), branch_computations={%region_15.16_spmd, %region_16.21_spmd} | conditional | flops 4409295872 | bytes 125304864 | solution.py:80
  151.7 6.3 %bitcast_dynamic-update-slice_fusion.1 = f32[2,1,8,512,128]{4,3,2,1,0:T(8,128)} fusion(f32[2,1,8,512,128]{4,3,2,1,0:T(8,128)} %get-tuple-element.675, f32[1,1,8,512,128]{4,3,2,1,0:T(8,128)S(1)} %slice.1306, f32[1024,512,8]{1,0,2:T(8,128)S(1)} %get-tuple-element.994, f32[8,512]{1,0:T(8,128)S(1)} %get-tuple-element.932, ...), kind=kOutput, calls=%fused_computation.123 | convolution fusion | flops 1095761920 | bytes 21790720 | tf_op jit(solution)/shard_map/cond/branch_1_fun/kgqw,wkd->kgqd/dot_general | solution.py:65
  165.6 7.3 %fusion.91 = f32[2,1,8,512,128]{4,3,2,1,0:T(8,128)} fusion(f32[2,1,8,512,128]{4,3,2,1,0:T(8,128)} %bitcast_dynamic-update-slice_fusion.1, f32[1024,512,8]{1,0,2:T(8,128)S(1)} %get-tuple-element.996, f32[8,512]{1,0:T(8,128)S(1)} %get-tuple-element.930, pred[512,1024]{0,1:T(8,128)(4,1)S(1)} %get-tuple-element.987, f32[8,512]{1,0:T(8,128)S(1)} %get-tuple-element.929, ...), kind=kOutput, calls=%fused_computation.122 | convolution fusion | flops 1095761920 | bytes 21790720 | tf_op jit(solution)/shard_map/cond/branch_1_fun/kgqw,wkd->kgqd/dot_general | solution.py:65
  177.0 32.4 %conditional.10 = ((f32[2,1,8,512]{3,2,1,0:T(8,128)S(1)}, f32[2,1,8,512]{3,2,1,0:T(8,128)S(1)}, f32[2,1,8,512,128]{4,3,2,1,0:T(8,128)})) conditional(s32[]{:T(128)} %convert_element_type.76, (f32[2,1,8,512]{3,2,1,0:T(8,128)S(1)}, f32[2,1,8,512]{3,2,1,0:T(8,128)S(1)}, f32[2,1,8,512,128]{4,3,2,1,0:T(8,128)}) %get-tuple-element.1110, ...), branch_computations={%region_21.22_spmd, %region_22.27_spmd} | conditional | flops 4409295872 | bytes 125304864 | solution.py:80
  198.0 7.3 %fusion.133 = f32[2,1,8,512,128]{4,3,2,1,0:T(8,128)} fusion(f32[2,1,8,512,128]{4,3,2,1,0:T(8,128)} %bitcast_dynamic-update-slice_fusion.2, f32[1024,512,8]{1,0,2:T(8,128)S(1)} %get-tuple-element.1012, f32[8,512]{1,0:T(8,128)S(1)} %get-tuple-element.934, pred[512,1024]{0,1:T(8,128)(4,1)S(1)} %get-tuple-element.1003, f32[8,512]{1,0:T(8,128)S(1)} %get-tuple-element.933, ...), kind=kOutput, calls=%fused_computation.178 | convolution fusion | flops 1095761920 | bytes 21790720 | tf_op jit(solution)/shard_map/cond/branch_1_fun/kgqw,wkd->kgqd/dot_general | solution.py:65
  210.4 32.1 %conditional.11 = ((f32[2,1,8,512]{3,2,1,0:T(8,128)S(1)}, f32[2,1,8,512]{3,2,1,0:T(8,128)S(1)}, f32[2,1,8,512,128]{4,3,2,1,0:T(8,128)})) conditional(s32[]{:T(128)} %convert_element_type.75, (f32[2,1,8,512]{3,2,1,0:T(8,128)S(1)}, f32[2,1,8,512]{3,2,1,0:T(8,128)S(1)}, f32[2,1,8,512,128]{4,3,2,1,0:T(8,128)}) %get-tuple-element.1111, ...), branch_computations={%region_27.28_spmd, %region_28.33_spmd} | conditional | flops 4409295872 | bytes 125304864 | solution.py:80
  231.2 7.3 %fusion.175 = f32[2,1,8,512,128]{4,3,2,1,0:T(8,128)} fusion(f32[2,1,8,512,128]{4,3,2,1,0:T(8,128)} %bitcast_dynamic-update-slice_fusion.3, f32[1024,512,8]{1,0,2:T(8,128)S(1)} %get-tuple-element.1028, f32[8,512]{1,0:T(8,128)S(1)} %get-tuple-element.938, pred[512,1024]{0,1:T(8,128)(4,1)S(1)} %get-tuple-element.1019, f32[8,512]{1,0:T(8,128)S(1)} %get-tuple-element.937, ...), kind=kOutput, calls=%fused_computation.234 | convolution fusion | flops 1095761920 | bytes 21790720 | tf_op jit(solution)/shard_map/cond/branch_1_fun/kgqw,wkd->kgqd/dot_general | solution.py:65
  242.5 33.8 %conditional.12 = ((f32[2,1,8,512]{3,2,1,0:T(8,128)S(1)}, f32[2,1,8,512]{3,2,1,0:T(8,128)S(1)}, f32[2,1,8,512,128]{4,3,2,1,0:T(8,128)})) conditional(s32[]{:T(128)} %convert_element_type.74, (f32[2,1,8,512]{3,2,1,0:T(8,128)S(1)}, f32[2,1,8,512]{3,2,1,0:T(8,128)S(1)}, f32[2,1,8,512,128]{4,3,2,1,0:T(8,128)}) %get-tuple-element.1112, ...), branch_computations={%region_33.34_spmd, %region_34.39_spmd} | conditional | flops 4409295872 | bytes 125304864 | solution.py:80
  249.4 7.3 %bitcast_dynamic-update-slice_fusion.4 = f32[2,1,8,512,128]{4,3,2,1,0:T(8,128)} fusion(f32[2,1,8,512,128]{4,3,2,1,0:T(8,128)} %get-tuple-element.702, f32[1,1,8,512,128]{4,3,2,1,0:T(8,128)S(1)} %slice.1343, f32[1024,512,8]{1,0,2:T(8,128)S(1)} %get-tuple-element.1042, f32[8,512]{1,0:T(8,128)S(1)} %get-tuple-element.944, ...), kind=kOutput, calls=%fused_computation.291 | convolution fusion | flops 1095761920 | bytes 21790720 | tf_op jit(solution)/shard_map/cond/branch_1_fun/kgqw,wkd->kgqd/dot_general | solution.py:65
  264.5 7.4 %fusion.217 = f32[2,1,8,512,128]{4,3,2,1,0:T(8,128)} fusion(f32[2,1,8,512,128]{4,3,2,1,0:T(8,128)} %bitcast_dynamic-update-slice_fusion.4, f32[1024,512,8]{1,0,2:T(8,128)S(1)} %get-tuple-element.1044, f32[8,512]{1,0:T(8,128)S(1)} %get-tuple-element.942, pred[512,1024]{0,1:T(8,128)(4,1)S(1)} %get-tuple-element.1035, f32[8,512]{1,0:T(8,128)S(1)} %get-tuple-element.941, ...), kind=kOutput, calls=%fused_computation.290 | convolution fusion | flops 1095761920 | bytes 21790720 | tf_op jit(solution)/shard_map/cond/branch_1_fun/kgqw,wkd->kgqd/dot_general | solution.py:65
  276.3 44.4 %conditional.13 = ((f32[2,1,8,512]{3,2,1,0:T(8,128)S(1)}, f32[2,1,8,512,128]{4,3,2,1,0:T(8,128)})) conditional(s32[]{:T(128)} %convert_element_type.73, (f32[2,1,8,512]{3,2,1,0:T(8,128)S(1)}, f32[2,1,8,512,128]{4,3,2,1,0:T(8,128)}) %tuple.221, (f32[2,1,8,512]{3,2,1,0:T(8,128)S(1)}, f32[2,1,8,512]{3,2,1,0:T(8,128)S(1)}, s32[]{:T(128)}, ...), branch_computations={%region_39.40_spmd, %region_40.45_spmd} | conditional | flops 4409295872 | bytes 125272088 | solution.py:80
  283.2 8.3 %fusion.246 = (f32[8,512]{1,0:T(8,128)S(1)}, f32[1024,512,8]{1,0,2:T(8,128)}) fusion(pred[512,1024]{0,1:T(8,128)(4,1)S(1)} %get-tuple-element.1050, bf16[2,512,1,8,128]{4,1,3,2,0:T(8,128)(2,1)S(1)} %copy.96, bf16[2,1024,128]{2,1,0:T(8,128)(2,1)} %get-tuple-element.708), kind=kOutput, calls=%fused_computation.334 | convolution fusion | flops 1086320640 | bytes 18628608 | tf_op jit(solution)/shard_map/cond/branch_1_fun/qkgd,wkd->kgqw/dot_general | solution.py:54
  291.5 9.7 %bitcast_dynamic-update-slice_fusion.5 = f32[2,1,8,512,128]{4,3,2,1,0:T(8,128)} fusion(f32[2,1,8,512,128]{4,3,2,1,0:T(8,128)} %get-tuple-element.710, f32[1,1,8,512,128]{4,3,2,1,0:T(8,128)S(1)} %slice.1357, f32[1024,512,8]{1,0,2:T(8,128)} %get-tuple-element.1058, f32[8,512]{1,0:T(8,128)S(1)} %get-tuple-element.1048, ...), kind=kOutput, calls=%fused_computation.351 | convolution fusion | flops 1095761920 | bytes 21790720 | tf_op jit(solution)/shard_map/cond/branch_1_fun/kgqw,wkd->kgqd/dot_general | solution.py:65
  301.2 7.9 %fusion.249 = f32[8,512]{1,0:T(8,128)S(1)} fusion(f32[1024,512,8]{1,0,2:T(8,128)} %get-tuple-element.1058, f32[8,512]{1,0:T(8,128)S(1)} %get-tuple-element.1048, pred[512,1024]{0,1:T(8,128)(4,1)S(1)} %get-tuple-element.1050), kind=kLoop, calls=%fused_computation.337 | loop fusion | flops 20967424 | bytes 17334272 | tf_op jit(solution)/shard_map/cond/branch_1_fun/reduce_sum | solution.py:64
  309.1 7.4 %fusion.263 = f32[2,1,8,512,128]{4,3,2,1,0:T(8,128)} fusion(f32[2,1,8,512,128]{4,3,2,1,0:T(8,128)} %bitcast_dynamic-update-slice_fusion.5, f32[1024,512,8]{1,0,2:T(8,128)S(1)} %get-tuple-element.1056, f32[8,512]{1,0:T(8,128)S(1)} %get-tuple-element.946, pred[512,1024]{0,1:T(8,128)(4,1)S(1)} %get-tuple-element.1049, f32[8,512]{1,0:T(8,128)S(1)} %get-tuple-element.945, ...), kind=kOutput, calls=%fused_computation.350 | convolution fusion | flops 1095761920 | bytes 21790720 | tf_op jit(solution)/shard_map/cond/branch_1_fun/kgqw,wkd->kgqd/dot_general | solution.py:65
  327.3 22.4 %all_to_all.71 = bf16[8,128,1024]{2,1,0:T(8,128)(2,1)S(1)} all-to-all(bf16[8,128,1024]{2,1,0:T(8,128)(2,1)} %convert_element_type.82), channel_id=1, replica_groups=mesh['ctx'=16,'head'=8] {'head'}, dimensions={0} | all-to-all | bytes 4194304 | tf_op jit(solution)/shard_map/all_to_all | solution.py:100
  (143 shorter events, 200.8 us)
Async XLA Ops:
  0.0 1.0 copy-start
  1.7 13.5 %all-to-all-start.1 = ((bf16[128,8,128]{2,0,1:T(8,128)(2,1)}), bf16[128,8,128]{2,0,1:T(8,128)(2,1)S(1)}, u32[]{:S(2)}, u32[]{:S(2)}) async-start(bf16[128,8,128]{2,0,1:T(8,128)(2,1)} %copy_bitcast_fusion.2), calls=%async_computation.1 | async-start | bytes 524288 | tf_op jit(solution)/shard_map/all_to_all | solution.py:24
  25.4 6.5 %collective-permute-start = (bf16[2,1024,128]{2,1,0:T(8,128)(2,1)S(1)}, bf16[2,1024,128]{2,1,0:T(8,128)(2,1)S(1)}, u32[]{:S(2)}, u32[]{:S(2)}) collective-permute-start(bf16[2,1024,128]{2,1,0:T(8,128)(2,1)S(1)} %pad_maximum_fusion.3), channel_id=1, source_target_pairs={{0,8},{8,16},{16,24},{24,32},{32,40},{40,48},{48,56},{56,64},{64,7... | collective-permute-start | bytes 1572872 | tf_op jit(solution)/shard_map/ppermute | solution.py:13
  31.9 10.5 %copy-start.5 = (bf16[2,1024,128]{2,1,0:T(8,128)(2,1)}, bf16[2,1024,128]{2,1,0:T(8,128)(2,1)S(1)}, u32[]{:S(2)}) copy-start(bf16[2,1024,128]{2,1,0:T(8,128)(2,1)S(1)} %collective-permute-done) | copy-start | bytes 1572868
  31.9 10.5 %collective-permute-start.1 = (bf16[2,1024,128]{2,1,0:T(8,128)(2,1)S(1)}, bf16[2,1024,128]{2,1,0:T(8,128)(2,1)S(1)}, u32[]{:S(2)}, u32[]{:S(2)}) collective-permute-start(bf16[2,1024,128]{2,1,0:T(8,128)(2,1)S(1)} %collective-permute-done), channel_id=1, source_target_pairs={{0,8},{8,16},{16,24},{24,32},{32,40},{40,48},{48,56},{56,64},{64,7... | collective-permute-start | bytes 1572872 | tf_op jit(solution)/shard_map/ppermute | solution.py:13
  42.4 29.4 %copy-start.4 = (bf16[2,1024,128]{2,1,0:T(8,128)(2,1)}, bf16[2,1024,128]{2,1,0:T(8,128)(2,1)S(1)}, u32[]{:S(2)}) copy-start(bf16[2,1024,128]{2,1,0:T(8,128)(2,1)S(1)} %collective-permute-done.1) | copy-start | bytes 1572868
  42.4 10.6 %collective-permute-start.2 = (bf16[2,1024,128]{2,1,0:T(8,128)(2,1)S(1)}, bf16[2,1024,128]{2,1,0:T(8,128)(2,1)}, u32[]{:S(2)}, u32[]{:S(2)}) collective-permute-start(bf16[2,1024,128]{2,1,0:T(8,128)(2,1)S(1)} %collective-permute-done.1), channel_id=1, source_target_pairs={{0,8},{8,16},{16,24},{24,32},{32,40},{40,48},{48,56},{56,64},{64,7... | collective-permute-start | bytes 1572872 | tf_op jit(solution)/shard_map/ppermute | solution.py:13
  46.8 32.0 %all-to-all-start = ((bf16[128,8,1024]{2,0,1:T(8,128)(2,1)}), bf16[128,8,1024]{2,0,1:T(8,128)(2,1)S(1)}, u32[]{:S(2)}, u32[]{:S(2)}) async-start(bf16[128,8,1024]{2,0,1:T(8,128)(2,1)} %bitcast.881), calls=%async_computation | async-start | bytes 4194304 | tf_op jit(solution)/shard_map/all_to_all | solution.py:23
  53.0 10.8 %collective-permute-start.3 = (bf16[2,1024,128]{2,1,0:T(8,128)(2,1)}, bf16[2,1024,128]{2,1,0:T(8,128)(2,1)}, u32[]{:S(2)}, u32[]{:S(2)}) collective-permute-start(bf16[2,1024,128]{2,1,0:T(8,128)(2,1)} %collective-permute-done.2), channel_id=1, source_target_pairs={{0,8},{8,16},{16,24},{24,32},{32,40},{40,48},{48,56},{56,64},{64,7... | collective-permute-start | bytes 1572872 | tf_op jit(solution)/shard_map/ppermute | solution.py:13
  63.8 10.8 %collective-permute-start.4 = (bf16[2,1024,128]{2,1,0:T(8,128)(2,1)}, bf16[2,1024,128]{2,1,0:T(8,128)(2,1)}, u32[]{:S(2)}, u32[]{:S(2)}) collective-permute-start(bf16[2,1024,128]{2,1,0:T(8,128)(2,1)} %collective-permute-done.3), channel_id=1, source_target_pairs={{0,8},{8,16},{16,24},{24,32},{32,40},{40,48},{48,56},{56,64},{64,7... | collective-permute-start | bytes 1572872 | tf_op jit(solution)/shard_map/ppermute | solution.py:13
  74.6 201.7 %collective-permute-start.5 = (bf16[2,1024,128]{2,1,0:T(8,128)(2,1)}, bf16[2,1024,128]{2,1,0:T(8,128)(2,1)}, u32[]{:S(2)}, u32[]{:S(2)}) collective-permute-start(bf16[2,1024,128]{2,1,0:T(8,128)(2,1)} %collective-permute-done.4), channel_id=1, source_target_pairs={{0,8},{8,16},{16,24},{24,32},{32,40},{40,48},{48,56},{56,64},{64,7... | collective-permute-start | bytes 1572872 | tf_op jit(solution)/shard_map/ppermute | solution.py:13
  78.8 1.3 copy-start.2
  116.0 3.6 %copy-start.7 = (bf16[1,1024,128]{2,1,0:T(8,128)(2,1)S(1)}, bf16[1,1024,128]{2,1,0:T(8,128)(2,1)}, u32[]{:S(2)}) copy-start(bf16[1,1024,128]{2,1,0:T(8,128)(2,1)} %get-tuple-element.667) | copy-start | bytes 786436 | tf_op jit(solution)/shard_map/cond
  144.8 32.2 %copy-start.3 = (bf16[1,1024,128]{2,1,0:T(8,128)(2,1)S(1)}, bf16[1,1024,128]{2,1,0:T(8,128)(2,1)}, u32[]{:S(2)}) copy-start(bf16[1,1024,128]{2,1,0:T(8,128)(2,1)} %get-tuple-element.1064) | copy-start | bytes 786436
  144.8 32.2 %copy-start.6 = (bf16[1,1024,128]{2,1,0:T(8,128)(2,1)S(1)}, bf16[1,1024,128]{2,1,0:T(8,128)(2,1)}, u32[]{:S(2)}) copy-start(bf16[1,1024,128]{2,1,0:T(8,128)(2,1)} %get-tuple-element.1063) | copy-start | bytes 786436
  320.7 35.4 %copy-start.1 = (bf16[128,1024]{1,0:T(8,128)(2,1)S(1)}, bf16[128,1024]{1,0:T(8,128)(2,1)}, u32[]{:S(2)}) copy-start(bf16[128,1024]{1,0:T(8,128)(2,1)} %param.101) | copy-start | bytes 786436
where the time goes:
time: 360 us; the launch traced here: 356 us
  matrix products  152 us (42%)
  other arithmetic  74 us (21%)
  local copies, waits for them, and re-layouts  38.4 us (11%)
  waiting for transfers between devices  34.4 us (10%)
  blocking collectives  32.5 us (9%)
  starting transfers between devices  17.1 us (5%)
  between operations  4.81 us (1%)
    dot_general x14, matrix products, update(): jnp.einsum('kgqw,wkd->kgqd', expo.astype(jnp.bfloat16), v_three, preferre...  97.3 us
    reduce_sum x14, other arithmetic, update(): den_new = den_all[index] * factor + jnp.sum(expo, axis=-1)  60 us
    dot_general x14, matrix products, update(): jnp.einsum('qkgd,wkd->kgqw', q_four[index], k_three, preferred_element_ty...  55.1 us
    ppermute x6, waiting for transfers between devices, from_behind(): return lax.ppermute(block, axis, route)  27.6 us
    all_to_all x1, blocking collectives, on_device(): lax.all_to_all(result, 'head', split_axis=0, concat_axis=1, tiled=True)  22.4 us
    slice x6, local copies, waits for them, and re-layouts, update(): acc_new = acc_all[index] * factor[..., None] + product  10.4 us
    all_to_all x1, blocking collectives, on_device(): lax.all_to_all(values, 'head', split_axis=1, concat_axis=0, tiled=True)  10.1 us
    ppermute x6, starting transfers between devices, from_behind(): return lax.ppermute(block, axis, route)  7.7 us
  transfers between devices with their start and end apart: 8, of which 6 were waited for; matrix products, arithmetic and copies ran while one was open for 57% of the time, Pallas kernels for 0%

commit v1 on v0

v1 whole, which is shorter than its diff:
```python
import functools

import jax
import jax.numpy as jnp
from jax import lax
from jax.experimental import pallas as pl
from jax.experimental.pallas import tpu as pltpu
from jax.sharding import PartitionSpec as P

MESH = pl.DeviceIdType.MESH
HEAD_DIM = 128
NDOCS = 8
NB = 16
BLK = 128
SPAN = 1024
QW = 512
KT = 256
SCALE2 = HEAD_DIM ** -0.5 * 1.4426950408889634
NEG = -1e30


def kv_head(c, j):
    return lax.rem(c // 8 + j // 4, 2) * 4 + lax.rem(c // 2, 4)


def remote(src, dst, send, recv, device):
    return pltpu.make_async_remote_copy(
        src_ref=src, dst_ref=dst, send_sem=send, recv_sem=recv, device_id=device, device_id_type=MESH
    )


def enter(peers):
    barrier = pltpu.get_barrier_semaphore()
    for peer in peers:
        pl.semaphore_signal(barrier, inc=1, device_id=peer, device_id_type=MESH)
    pl.semaphore_wait(barrier, len(peers))


def ctx_peers(c):
    core, z, y = lax.rem(c, 2), lax.rem(c // 2, 4), c // 8
    order = [(dz, dy, dc) for dy, dc in ((0, 0), (1, 1), (1, 0), (0, 1)) for dz in (2, 1, 3, 0)]
    return [
        lax.rem(y + dy, 2) * 8 + lax.rem(z + dz, 4) * 2 + lax.rem(core + dc, 2)
        for dz, dy, dc in order
        if (dz, dy, dc) != (0, 0, 0)
    ]


def gather_kernel(q_ref, k_ref, v_ref, qg_ref, kv_ref, loc, s_q, r_q, s_1, r_1, s_g, r_g, s_b, r_b, own):
    c, j = lax.axis_index("ctx"), lax.axis_index("head")
    core, x, y = lax.rem(c, 2), lax.rem(j, 4), j // 4
    sibling = {"ctx": c + 1 - 2 * core, "head": j}
    across = {"ctx": lax.rem(c + 8, 16), "head": lax.rem(j + 4, 8)}
    right = {"ctx": c, "head": y * 4 + lax.rem(x + 1, 4)}
    left = {"ctx": c, "head": y * 4 + lax.rem(x + 3, 4)}
    others = ctx_peers(c)
    for h in range(8):
        loc[0, h] = k_ref[:, h * 128 : (h + 1) * 128]
        loc[1, h] = v_ref[:, h * 128 : (h + 1) * 128].T
    enter([{"ctx": o, "head": j} for o in others] + [across, right, left])

    ends = []
    for n, o in enumerate(others):
        cp = remote(
            loc.at[lax.rem(o, 2), kv_head(o, j)], kv_ref.at[lax.rem(o, 2), c, j],
            s_1.at[n], r_1.at[n], {"ctx": o, "head": j},
        )
        cp.start()
        ends.append(cp)
    mine = pltpu.make_async_copy(loc.at[core, kv_head(c, j)], kv_ref.at[core, c, j], own.at[0])
    mine.start()
    q_ends = []
    for n, o in enumerate(others):
        columns = kv_head(o, j) * 1024 + lax.rem(o, 2) * QW
        cp = remote(
            q_ref.at[:, pl.ds(pl.multiple_of(columns, QW), QW)], qg_ref.at[c],
            s_q.at[n], r_q.at[n], {"ctx": o, "head": j},
        )
        cp.start()
        q_ends.append(cp)
    columns = kv_head(c, j) * 1024 + core * QW
    mine_q = pltpu.make_async_copy(q_ref.at[:, pl.ds(pl.multiple_of(columns, QW), QW)], qg_ref.at[c], own.at[1])
    mine_q.start()
    mine.wait()
    for cp in ends:
        cp.wait_recv()

    def slot(dx, dy, half=None):
        place = lax.rem(y + dy, 2) * 4 + lax.rem(x + dx, 4)
        if half is None:
            return kv_ref.at[core, :, place]
        return kv_ref.at[core, pl.ds(half * 8, 8), place]

    count = [0]
    to_sibling = []

    def go(ref, device):
        cp = remote(ref, ref, s_g.at[count[0]], r_g.at[count[0]], device)
        count[0] += 1
        cp.start()
        return cp

    def give(ref):
        n = len(to_sibling)
        cp = remote(ref, ref, s_b.at[n], r_b.at[n], sibling)
        cp.start()
        to_sibling.append(cp)

    hops = []
    over = go(slot(0, 0), across)
    first = [(go(slot(0, 0), right), go(slot(0, 0), left))]
    give(slot(0, 0))
    over.wait_recv()
    first.append((go(slot(0, 1), right), go(slot(0, 1), left)))
    give(slot(0, 1))
    second = []
    for dy in (0, 1):
        from_left, from_right = first[dy]
        from_left.wait_recv()
        a = go(slot(3, dy, 0), right)
        give(slot(3, dy))
        from_right.wait_recv()
        b = go(slot(1, dy, 1), left)
        give(slot(1, dy))
        second.append((a, b))
        hops += [from_left, from_right, a, b]
    for dy in (0, 1):
        a, b = second[dy]
        a.wait_recv()
        b.wait_recv()
        give(slot(2, dy))
    mine_q.wait()
    for cp in q_ends:
        cp.wait()
    for cp in ends + [over] + hops:
        cp.wait_send()
    for cp in to_sibling:
        cp.wait()


def gather(q, k, v):
    dma = pltpu.SemaphoreType.DMA
    anywhere, vmem = pl.BlockSpec(memory_space=pl.ANY), pl.BlockSpec(memory_space=pltpu.VMEM)
    return pl.pallas_call(
        gather_kernel,
        out_shape=(
            jax.ShapeDtypeStruct((NB, BLK, QW), jnp.bfloat16),
            jax.ShapeDtypeStruct((2, NB, 8, BLK, HEAD_DIM), jnp.bfloat16),
        ),
        in_specs=[anywhere, vmem, vmem],
        out_specs=(anywhere, anywhere),
        scratch_shapes=[
            pltpu.VMEM((2, 8, BLK, HEAD_DIM), jnp.bfloat16),
            dma((15,)), dma((15,)), dma((15,)), dma((15,)), dma((9,)), dma((9,)), dma((8,)), dma((8,)), dma((2,)),
        ],
        compiler_params=pltpu.CompilerParams(collective_id=0, has_side_effects=True),
    )(q, k, v)


def attend_kernel(lengths, q_ref, kv_ref, o_ref, m_ref, a_ref, st_ref, lo_ref, s0, s1, p0, p1, al0, al1):
    sb, pb, ab = (s0, s1), (p0, p1), (al0, al1)
    core, j = lax.rem(lax.axis_index("ctx"), 2), lax.axis_index("head")
    halves, width = 2, QW // 2
    m_ref[...] = jnp.full(m_ref.shape, NEG, jnp.float32)
    a_ref[...] = jnp.zeros(a_ref.shape, jnp.float32)
    p1[...] = jnp.zeros(p1.shape, jnp.bfloat16)
    al1[...] = jnp.zeros(al1.shape, jnp.float32)
    total = jnp.int32(0)
    for i in range(NB):
        p = i * SPAN + j * BLK
        row = lax.broadcasted_iota(jnp.int32, (1, BLK), 1) + p
        start, low, end = jnp.zeros((1, BLK), jnp.int32), jnp.int32(0), jnp.int32(0)
        for d in range(NDOCS - 1):
            end = end + lengths[d]
            start = jnp.where(row >= end, end, start)
            low = jnp.where(p >= end, end, low)
        st_ref[i] = start
        lo_ref[i] = low
        total = total + (p + BLK - low + KT - 1) // KT

    def after(b, top):
        low = top - KT
        done = low <= lo_ref[b]
        following = jnp.minimum(b + 1, NB - 1)
        finished = (done & (b + 1 >= NB)) | (top < 0)
        new_top = jnp.where(done, following * SPAN + j * BLK + BLK, low)
        return jnp.where(done, following, b), jnp.where(finished, -1, new_top)

    def first_block(top):
        return jnp.maximum(top - KT, 0) // BLK

    def scores(b, top, s_ref, n):
        k = kv_ref[0, pl.ds(first_block(top), KT // BLK)].reshape(KT, HEAD_DIM)
        q = jnp.concatenate([q_ref[b, :, h * 128 : (h + 1) * 128] for h in (2 * n, 2 * n + 1)], 0)
        s_ref[:, n * width : (n + 1) * width] = lax.dot_general(
            k, q, (((1,), (1,)), ((), ())), preferred_element_type=jnp.float32
        )

    def visible(b, top):
        k_first = first_block(top) * BLK
        row = lax.broadcasted_iota(jnp.int32, (1, BLK), 1) + (b * SPAN + j * BLK)
        last = jnp.minimum(row, top - 1) - k_first
        place = lax.broadcasted_iota(jnp.int32, (KT, BLK), 0)
        return (place >= st_ref[b] - k_first) & (place <= last)

    def weights(b, s_ref, p_ref, f_ref, n, seen):
        part = slice(n * width, (n + 1) * width)
        s = s_ref[:, part]
        s = jnp.concatenate([jnp.where(seen, s[:, h * 128 : (h + 1) * 128], NEG) for h in (0, 1)], 1)
        old = m_ref[b, :, part]
        new = jnp.maximum(old, jnp.max(s, axis=0, keepdims=True))
        p_ref[:, part] = jnp.exp2((s - new) * SCALE2).astype(jnp.bfloat16)
        f_ref[:, part] = jnp.exp2((old - new) * SCALE2)
        m_ref[b, :, part] = new

    def mix(b, top, p_ref, f_ref, n):
        part = slice(n * width, (n + 1) * width)
        base = first_block(top)
        vt = jnp.concatenate([kv_ref[1, base + t] for t in range(KT // BLK)], 1)
        vt = jnp.concatenate([vt, jnp.ones((16, KT), jnp.bfloat16)], 0)
        product = jnp.dot(vt, p_ref[:, part], preferred_element_type=jnp.float32)
        a_ref[b, :, part] = a_ref[b, :, part] * f_ref[:, part] + product

    b0, top0 = jnp.int32(0), j * BLK + BLK
    for n in range(halves):
        scores(b0, top0, sb[0], n)

    def body(_, carry):
        b_old, top_old, b, top = carry
        for u in range(4):
            now, other = u % 2, (u + 1) % 2
            b_new, top_new = after(b, top)
            seen = visible(b, top)
            for n in range(halves):
                scores(b_new, top_new, sb[other], n)
                weights(b, sb[now], pb[now], ab[now], n, seen)
                mix(b_old, top_old, pb[other], ab[other], n)
            b_old, top_old, b, top = b, top, b_new, top_new
        return b_old, top_old, b, top

    lax.fori_loop(0, (total + 4) // 4, body, (b0, top0, b0, top0))

    def finish(i, _):
        out = a_ref[i, 0:128] / a_ref[i, 128:129]
        for h in range(4):
            o_ref[i, :, h * 128 : (h + 1) * 128] = out[:, h * 128 : (h + 1) * 128].T.astype(jnp.bfloat16)
        return 0

    lax.fori_loop(0, NB, finish, 0)


def attend(lengths, q, kv):
    f32, vmem = jnp.float32, pltpu.VMEM
    return pl.pallas_call(
        attend_kernel,
        out_shape=jax.ShapeDtypeStruct((NB, BLK, QW), jnp.bfloat16),
        grid_spec=pltpu.PrefetchScalarGridSpec(
            num_scalar_prefetch=1,
            grid=(),
            in_specs=[pl.BlockSpec(memory_space=vmem)] * 2,
            out_specs=pl.BlockSpec(memory_space=vmem),
            scratch_shapes=[
                vmem((NB, 1, QW), f32),
                vmem((NB, 144, QW), f32),
                vmem((NB, 1, BLK), jnp.int32),
                pltpu.SMEM((NB,), jnp.int32),
                vmem((KT, QW), f32),
                vmem((KT, QW), f32),
                vmem((KT, QW), jnp.bfloat16),
                vmem((KT, QW), jnp.bfloat16),
                vmem((1, QW), f32),
                vmem((1, QW), f32),
            ],
        ),
        compiler_params=pltpu.CompilerParams(vmem_limit_bytes=48 * 2**20),
    )(lengths, q, kv)


def return_kernel(o_ref, out_ref, send, recv, own):
    c, j = lax.axis_index("ctx"), lax.axis_index("head")
    others = ctx_peers(c)
    enter([{"ctx": o, "head": j} for o in others])
    columns = pl.ds(pl.multiple_of(kv_head(c, j) * 1024 + lax.rem(c, 2) * QW, QW), QW)
    ends = []
    for n, o in enumerate(others):
        cp = remote(o_ref.at[o], out_ref.at[:, columns], send.at[n], recv.at[n], {"ctx": o, "head": j})
        cp.start()
        ends.append(cp)
    mine = pltpu.make_async_copy(o_ref.at[c], out_ref.at[:, columns], own)
    mine.start()
    mine.wait()
    for cp in ends:
        cp.wait()


def give_back(o):
    dma = pltpu.SemaphoreType.DMA
    anywhere = pl.BlockSpec(memory_space=pl.ANY)
    return pl.pallas_call(
        return_kernel,
        out_shape=jax.ShapeDtypeStruct((BLK, 64 * HEAD_DIM), jnp.bfloat16),
        in_specs=[anywhere],
        out_specs=anywhere,
        scratch_shapes=[dma((15,)), dma((15,)), dma],
        compiler_params=pltpu.CompilerParams(collective_id=1, has_side_effects=True),
    )(o)


def on_device(queries, keys, values, doc_lengths):
    q, kv = gather(queries, keys, values)
    o = attend(doc_lengths, q, kv.reshape(2, NB * 8, BLK, HEAD_DIM))
    return give_back(o)


def solution(mesh):
    rows = P(("ctx", "head"), None)
    return jax.shard_map(on_device, mesh=mesh, in_specs=(rows, rows, rows, P()), out_specs=rows, check_vma=False)
```

time: 360 us -> 133 us (0.37)
  the two profiles are of different devices: /device:TPU:105 before, /device:TPU:17 now
where the time goes in v1:
time: 133 us; the launch traced here: 131 us
  Pallas kernels  125 us (94%)
  local copies, waits for them, and re-layouts  6 us (5%)
    pallas_call x1, Pallas kernels, gather(): pl.pallas_call(gather_kernel, out_shape=(jax.ShapeDtypeStruct((NB, BLK, Q...  55.1 us
    pallas_call x1, Pallas kernels, attend(): pl.pallas_call(attend_kernel, out_shape=jax.ShapeDtypeStruct((NB, BLK, QW...  40.5 us
    pallas_call x1, Pallas kernels, give_back(): pl.pallas_call(return_kernel, out_shape=jax.ShapeDtypeStruct((BLK, 64 * H...  29.1 us
    unnamed x7, local copies, waits for them, and re-layouts  6 us

profile of v1, /device:TPU:17, one launch (start us, length us, event | category | flops | bytes accessed | tf_op | source)
XLA Modules:
  0.0 130.8 jit_solution(18247965634400202336)
XLA Ops:
  0.0 0.0 copy-start.2
  0.0 55.1 %shard_map.46 = (bf16[16,128,512]{2,1,0:T(8,128)(2,1)}, bf16[2,16,8,128,128]{4,3,2,1,0:T(8,128)(2,1)}) custom-call(bf16[128,8192]{1,0:T(8,128)(2,1)} %q_ref.1, bf16[128,1024]{1,0:T(8,128)(2,1)} %k_ref.1, bf16[128,1024]{1,0:T(8,128)(2,1)} %v_ref.1), custom_call_target="tpu_custom_call" | custom-call | tf_op jit(solution)/shard_map/pallas_call | solution.py:144
  55.1 0.0 copy-done.2
  55.1 0.0 copy-start.1
  55.1 1.6 %copy-done.1 = bf16[16,128,512]{2,1,0:T(8,128)(2,1)S(1)} copy-done((bf16[16,128,512]{2,1,0:T(8,128)(2,1)S(1)}, bf16[16,128,512]{2,1,0:T(8,128)(2,1)}, u32[]{:S(2)}) %copy-start.1) | copy-done | bytes 2097176
  56.7 40.5 %shard_map.47.o_ref = bf16[16,128,512]{2,1,0:T(8,128)(2,1)S(1)} custom-call(s32[8]{0:T(128)S(1)} %copy-done.2, bf16[16,128,512]{2,1,0:T(8,128)(2,1)S(1)} %copy-done.1, bf16[2,128,128,128]{3,2,1,0:T(8,128)(2,1)} %bitcast.1), custom_call_target="tpu_custom_call" | custom-call | tf_op jit(solution)/shard_map/pallas_call | solution.py:254
  97.2 0.0 copy-start
  97.2 1.3 %copy-done = bf16[16,128,512]{2,1,0:T(8,128)(2,1)} copy-done((bf16[16,128,512]{2,1,0:T(8,128)(2,1)}, bf16[16,128,512]{2,1,0:T(8,128)(2,1)S(1)}, u32[]{:S(2)}) %copy-start) | copy-done | bytes 2097176
  98.5 29.1 %shard_map.48 = bf16[128,8192]{1,0:T(8,128)(2,1)} custom-call(bf16[16,128,512]{2,1,0:T(8,128)(2,1)} %copy-done), custom_call_target="tpu_custom_call" | custom-call | tf_op jit(solution)/shard_map/pallas_call | solution.py:299
  127.7 3.1 %copy.6 = bf16[128,8192]{1,0:T(8,128)(2,1)} copy(bf16[128,8192]{1,0:T(8,128)(2,1)} %shard_map.48) | data formatting | bytes 4194304
Async XLA Ops:
  0.0 55.1 %copy-start.2 = (s32[8]{0:T(128)S(1)}, s32[8]{0:T(128)}, u32[]{:S(2)}) copy-start(s32[8]{0:T(128)} %lengths.1) | copy-start | bytes 100
  55.1 1.6 %copy-start.1 = (bf16[16,128,512]{2,1,0:T(8,128)(2,1)S(1)}, bf16[16,128,512]{2,1,0:T(8,128)(2,1)}, u32[]{:S(2)}) copy-start(bf16[16,128,512]{2,1,0:T(8,128)(2,1)} %get-tuple-element.7.q_ref) | copy-start | bytes 6291460
  97.2 1.3 %copy-start = (bf16[16,128,512]{2,1,0:T(8,128)(2,1)}, bf16[16,128,512]{2,1,0:T(8,128)(2,1)S(1)}, u32[]{:S(2)}) copy-start(bf16[16,128,512]{2,1,0:T(8,128)(2,1)S(1)} %shard_map.47.o_ref) | copy-start | bytes 6291460

commit v2 on v1

v2 whole, which is shorter than its diff:
```python
import functools

import jax
import jax.numpy as jnp
from jax import lax
from jax.experimental import pallas as pl
from jax.experimental.pallas import tpu as pltpu
from jax.sharding import PartitionSpec as P

MESH = pl.DeviceIdType.MESH
HEAD_DIM = 128
NDOCS = 8
NB = 16
BLK = 128
SPAN = 1024
QW = 512
KT = 512
DIAG = 4
SCALE2 = HEAD_DIM ** -0.5 * 1.4426950408889634
NEG = -1e30


def kv_head(c, j):
    return lax.rem(c // 8 + j // 4, 2) * 4 + lax.rem(c // 2, 4)


def remote(src, dst, send, recv, device):
    return pltpu.make_async_remote_copy(
        src_ref=src, dst_ref=dst, send_sem=send, recv_sem=recv, device_id=device, device_id_type=MESH
    )


def enter(peers):
    barrier = pltpu.get_barrier_semaphore()
    for peer in peers:
        pl.semaphore_signal(barrier, inc=1, device_id=peer, device_id_type=MESH)
    pl.semaphore_wait(barrier, len(peers))


def ctx_peers(c):
    core, z, y = lax.rem(c, 2), lax.rem(c // 2, 4), c // 8
    order = [(dz, dy, dc) for dy, dc in ((0, 0), (1, 1), (1, 0), (0, 1)) for dz in (2, 1, 3, 0)]
    return [
        lax.rem(y + dy, 2) * 8 + lax.rem(z + dz, 4) * 2 + lax.rem(core + dc, 2)
        for dz, dy, dc in order
        if (dz, dy, dc) != (0, 0, 0)
    ]


def gather_kernel(q_ref, k_ref, v_ref, qg_ref, kv_ref, loc, s_q, r_q, s_1, r_1, s_g, r_g, s_b, r_b, own):
    c, j = lax.axis_index("ctx"), lax.axis_index("head")
    core, x, y = lax.rem(c, 2), lax.rem(j, 4), j // 4
    sibling = {"ctx": c + 1 - 2 * core, "head": j}
    across = {"ctx": lax.rem(c + 8, 16), "head": lax.rem(j + 4, 8)}
    right = {"ctx": c, "head": y * 4 + lax.rem(x + 1, 4)}
    left = {"ctx": c, "head": y * 4 + lax.rem(x + 3, 4)}
    others = ctx_peers(c)
    for h in range(8):
        loc[0, h] = k_ref[:, h * 128 : (h + 1) * 128]
        loc[1, h] = v_ref[:, h * 128 : (h + 1) * 128].T
    enter([{"ctx": o, "head": j} for o in others] + [across, right, left])

    ends = []
    for n, o in enumerate(others):
        cp = remote(
            loc.at[lax.rem(o, 2), kv_head(o, j)], kv_ref.at[lax.rem(o, 2), c, j],
            s_1.at[n], r_1.at[n], {"ctx": o, "head": j},
        )
        cp.start()
        ends.append(cp)
    mine = pltpu.make_async_copy(loc.at[core, kv_head(c, j)], kv_ref.at[core, c, j], own.at[0])
    mine.start()
    columns = kv_head(c, j) * 1024 + core * QW
    mine_q = pltpu.make_async_copy(q_ref.at[:, pl.ds(pl.multiple_of(columns, QW), QW)], qg_ref.at[c], own.at[1])
    mine_q.start()
    mine.wait()
    for cp in ends:
        cp.wait_recv()

    def part(dx, dy, first, size):
        place = lax.rem(y + dy, 2) * 4 + lax.rem(x + dx, 4)
        return kv_ref.at[core, pl.ds(first, size), place]

    moves, to_sibling = [], []

    def go(ref, device):
        n = len(moves)
        cp = remote(ref, ref, s_g.at[n], r_g.at[n], device)
        cp.start()
        moves.append(cp)
        return cp

    def give(ref):
        n = len(to_sibling)
        cp = remote(ref, ref, s_b.at[n], r_b.at[n], sibling)
        cp.start()
        to_sibling.append(cp)

    a_over = go(part(0, 0, 0, 8), across)
    a_right, a_left = go(part(0, 0, 0, 8), right), go(part(0, 0, 0, 8), left)
    b_right, b_left = go(part(0, 0, 8, 8), right), go(part(0, 0, 8, 8), left)
    b_over = go(part(0, 0, 8, 8), across)
    give(part(0, 0, 0, 16))
    q_ends = []
    for n, o in enumerate(others):
        columns = kv_head(o, j) * 1024 + lax.rem(o, 2) * QW
        cp = remote(
            q_ref.at[:, pl.ds(pl.multiple_of(columns, QW), QW)], qg_ref.at[c],
            s_q.at[n], r_q.at[n], {"ctx": o, "head": j},
        )
        cp.start()
        q_ends.append(cp)
    a_over.wait_recv()
    c_right, c_left = go(part(0, 1, 0, 8), right), go(part(0, 1, 0, 8), left)
    a_right.wait_recv()
    a_far_right = go(part(3, 0, 0, 4), right)
    a_left.wait_recv()
    a_far_left = go(part(1, 0, 4, 4), left)
    b_right.wait_recv()
    b_far_right = go(part(3, 0, 8, 4), right)
    b_over_3 = go(part(3, 0, 8, 8), across)
    give(part(3, 0, 0, 16))
    b_left.wait_recv()
    b_far_left = go(part(1, 0, 12, 4), left)
    b_over_1 = go(part(1, 0, 8, 8), across)
    give(part(1, 0, 0, 16))
    b_over.wait_recv()
    give(part(0, 1, 0, 16))
    c_right.wait_recv()
    c_far_right = go(part(3, 1, 0, 4), right)
    c_left.wait_recv()
    c_far_left = go(part(1, 1, 4, 4), left)
    b_far_right.wait_recv()
    b_far_left.wait_recv()
    b_over_2 = go(part(2, 0, 8, 8), across)
    a_far_right.wait_recv()
    a_far_left.wait_recv()
    give(part(2, 0, 0, 16))
    b_over_3.wait_recv()
    give(part(3, 1, 0, 16))
    b_over_1.wait_recv()
    give(part(1, 1, 0, 16))
    c_far_right.wait_recv()
    c_far_left.wait_recv()
    b_over_2.wait_recv()
    give(part(2, 1, 0, 16))
    mine_q.wait()
    for cp in q_ends:
        cp.wait()
    for cp in ends + moves:
        cp.wait_send()
    for cp in to_sibling:
        cp.wait()


def gather(q, k, v):
    dma = pltpu.SemaphoreType.DMA
    anywhere, vmem = pl.BlockSpec(memory_space=pl.ANY), pl.BlockSpec(memory_space=pltpu.VMEM)
    return pl.pallas_call(
        gather_kernel,
        out_shape=(
            jax.ShapeDtypeStruct((NB, BLK, QW), jnp.bfloat16),
            jax.ShapeDtypeStruct((2, NB, 8, BLK, HEAD_DIM), jnp.bfloat16),
        ),
        in_specs=[anywhere, vmem, vmem],
        out_specs=(anywhere, anywhere),
        scratch_shapes=[
            pltpu.VMEM((2, 8, BLK, HEAD_DIM), jnp.bfloat16),
            dma((15,)), dma((15,)), dma((15,)), dma((15,)), dma((17,)), dma((17,)), dma((8,)), dma((8,)), dma((2,)),
        ],
        compiler_params=pltpu.CompilerParams(collective_id=0, has_side_effects=True),
    )(q, k, v)


def attend_kernel(
    lengths, q_hbm, kv_ref, o_hbm, q_ref, o_ref, kd, vd, kb, vb, ka, qa, m_ref, a_ref, lo_ref, next_ref,
    s0, s1, p0, p1, f0, f1, x0, x1, load, store,
):
    sb, pb, fb, xb = (s0, s1), (p0, p1), (f0, f1), (x0, x1)
    j = lax.axis_index("head")
    bf = jnp.bfloat16
    copies = [
        pltpu.make_async_copy(q_hbm, q_ref, load.at[0]),
        pltpu.make_async_copy(kv_ref.at[0, :, j], kd, load.at[1]),
        pltpu.make_async_copy(kv_ref.at[1, :, j], vd, load.at[2]),
        pltpu.make_async_copy(kv_ref.at[0], kb.at[pl.ds(1, NB)], load.at[3]),
        pltpu.make_async_copy(kv_ref.at[1], vb.at[pl.ds(1, NB)], load.at[4]),
    ]
    for cp in copies:
        cp.start()

    lane = lax.broadcasted_iota(jnp.int32, (1, BLK), 1)
    first, last, end, ends = jnp.zeros((1, BLK), jnp.int32), jnp.full((1, BLK), 1 << 30, jnp.int32), jnp.int32(0), []
    for d in range(NDOCS):
        first = jnp.where(lane == d, end, first)
        end = end + lengths[d]
        ends.append(end)
        last = jnp.where(lane == d, end, last)
    place = lax.broadcasted_iota(jnp.int32, (BLK, BLK), 0)
    kb[0] = jnp.zeros(kb.shape[1:], bf)
    vb[0] = jnp.zeros(vb.shape[1:], bf)
    ka[0] = jnp.full(ka.shape[1:], NEG, bf)

    def mark(i, _):
        for t in range(8):
            row = place + (i * SPAN + t * BLK)
            ka[i + 1, t] = jnp.where((row >= first) & (row < last), 0.0, NEG).astype(bf)
        return 0

    lax.fori_loop(0, NB, mark, 0)
    total = jnp.int32(0)
    for i in range(NB):
        p = i * SPAN + j * BLK
        row = place + p
        qa[i] = jnp.where((row >= first) & (row < last), 1.0, 0.0).astype(bf)
        low = jnp.int32(0)
        for d in range(NDOCS - 1):
            low = jnp.where(p >= ends[d], ends[d], low)
        lo_ref[i] = low
        total = total + (p - low + KT - 1) // KT
    follow = jnp.int32(NB - 1)
    for i in range(NB - 1, -1, -1):
        next_ref[i] = follow
        follow = jnp.where(i * SPAN + j * BLK > lo_ref[i], i, follow)
    p1[...] = jnp.zeros(p1.shape, bf)
    f1[...] = jnp.ones(f1.shape, jnp.float32)

    def queries(b):
        marks = qa[b]
        return jnp.concatenate(
            [jnp.concatenate([q_ref[b, :, h * 128 : (h + 1) * 128], marks], 1) for h in range(4)], 0
        )

    def product(k, q):
        return lax.dot_general(k, q, (((1,), (1,)), ((), ())), preferred_element_type=jnp.float32)

    def with_ones(vt):
        return jnp.concatenate([vt, jnp.ones((16, vt.shape[1]), bf)], 0)

    for cp in copies[:3]:
        cp.wait()
    below = place <= lax.broadcasted_iota(jnp.int32, (BLK, BLK), 1)

    def diagonal(g, _):
        blocks = [g * DIAG + u for u in range(DIAG)]
        scores = []
        for b in blocks:
            s = product(jnp.concatenate([kd[b], ka[b + 1, j]], 1), queries(b))
            scores.append(jnp.concatenate([jnp.where(below, s[:, h * 128 : (h + 1) * 128], NEG) for h in range(4)], 1))
        parts = []
        for b, s in zip(blocks, scores):
            top = jnp.max(s, axis=0, keepdims=True)
            m_ref[b] = top
            parts.append(jnp.exp2((s - top) * SCALE2).astype(bf))
        for b, p in zip(blocks, parts):
            a_ref[b] = jnp.dot(with_ones(vd[b]), p, preferred_element_type=jnp.float32)
        return 0

    lax.fori_loop(0, NB // DIAG, diagonal, 0)
    for cp in copies[3:]:
        cp.wait()

    kf, af, vf = (r.reshape((NB + 1) * 8, BLK, HEAD_DIM) for r in (kb, ka, vb))
    steps = KT // BLK

    def after(b, top):
        low = top - KT
        done = low <= lo_ref[b]
        b_new = jnp.where(done, next_ref[b], b)
        over = (done & (b_new <= b)) | (top <= 0)
        return b_new, jnp.where(over, 0, jnp.where(done, b_new * SPAN + j * BLK, low))

    def window(top):
        return (jnp.maximum(top, 0) - KT + SPAN) // BLK

    def score(b, top, s_ref, x_ref):
        at = pl.ds(window(top), steps)
        k = jnp.concatenate([kf[at].reshape(KT, HEAD_DIM), af[at].reshape(KT, BLK)], 1)
        s = product(k, queries(b))
        s_ref[...] = s
        x_ref[...] = jnp.max(s, axis=0, keepdims=True)

    def weigh(b, s_ref, x_ref, p_ref, f_ref):
        old = m_ref[b]
        new = jnp.maximum(old, x_ref[...])
        p_ref[...] = jnp.exp2((s_ref[...] - new) * SCALE2).astype(bf)
        f_ref[...] = jnp.exp2((old - new) * SCALE2)
        m_ref[b] = new

    def mix(b, top, p_ref, f_ref):
        at = window(top)
        vt = jnp.concatenate([vf[at + t] for t in range(steps)], 1)
        a_ref[b] = a_ref[b] * f_ref[...] + jnp.dot(with_ones(vt), p_ref[...], preferred_element_type=jnp.float32)

    b0, top0 = follow, follow * SPAN + j * BLK
    score(b0, top0, sb[0], xb[0])

    def body(_, carry):
        b_old, top_old, b, top = carry
        for u in range(4):
            now, other = u % 2, (u + 1) % 2
            b_new, top_new = after(b, top)
            weigh(b, sb[now], xb[now], pb[now], fb[now])
            mix(b_old, top_old, pb[other], fb[other])
            score(b_new, top_new, sb[other], xb[other])
            b_old, top_old, b, top = b, top, b_new, top_new
        return b_old, top_old, b, top

    lax.fori_loop(0, jnp.where(total > 0, (total + 4) // 4, 0), body, (b0, top0, b0, top0))

    def finish(i, _):
        out = a_ref[i, 0:128] * (1.0 / a_ref[i, 128:129])
        for h in range(4):
            o_ref[i, :, h * 128 : (h + 1) * 128] = out[:, h * 128 : (h + 1) * 128].T.astype(bf)
        pltpu.make_async_copy(o_ref.at[i], o_hbm.at[i], store.at[i]).start()
        return 0

    lax.fori_loop(0, NB, finish, 0)
    for i in range(NB):
        pltpu.make_async_copy(o_ref.at[i], o_hbm.at[i], store.at[i]).wait()


def attend(lengths, q, kv):
    f32, bf, vmem = jnp.float32, jnp.bfloat16, pltpu.VMEM
    anywhere = pl.BlockSpec(memory_space=pl.ANY)
    return pl.pallas_call(
        attend_kernel,
        out_shape=jax.ShapeDtypeStruct((NB, BLK, QW), bf),
        grid_spec=pltpu.PrefetchScalarGridSpec(
            num_scalar_prefetch=1,
            grid=(),
            in_specs=[anywhere] * 2,
            out_specs=anywhere,
            scratch_shapes=[
                vmem((NB, BLK, QW), bf),
                vmem((NB, BLK, QW), bf),
                vmem((NB, BLK, HEAD_DIM), bf),
                vmem((NB, HEAD_DIM, BLK), bf),
                vmem((NB + 1, 8, BLK, HEAD_DIM), bf),
                vmem((NB + 1, 8, HEAD_DIM, BLK), bf),
                vmem((NB + 1, 8, BLK, BLK), bf),
                vmem((NB, BLK, BLK), bf),
                vmem((NB, 1, QW), f32),
                vmem((NB, 144, QW), f32),
                pltpu.SMEM((NB,), jnp.int32),
                pltpu.SMEM((NB,), jnp.int32),
                vmem((KT, QW), f32),
                vmem((KT, QW), f32),
                vmem((KT, QW), bf),
                vmem((KT, QW), bf),
                vmem((1, QW), f32),
                vmem((1, QW), f32),
                vmem((1, QW), f32),
                vmem((1, QW), f32),
                pltpu.SemaphoreType.DMA((5,)),
                pltpu.SemaphoreType.DMA((NB,)),
            ],
        ),
        compiler_params=pltpu.CompilerParams(vmem_limit_bytes=56 * 2**20),
    )(lengths, q, kv)


def return_kernel(o_ref, out_ref, send, recv, own):
    c, j = lax.axis_index("ctx"), lax.axis_index("head")
    others = ctx_peers(c)
    enter([{"ctx": o, "head": j} for o in others])
    columns = pl.ds(pl.multiple_of(kv_head(c, j) * 1024 + lax.rem(c, 2) * QW, QW), QW)
    ends = []
    for n, o in enumerate(others):
        cp = remote(o_ref.at[o], out_ref.at[:, columns], send.at[n], recv.at[n], {"ctx": o, "head": j})
        cp.start()
        ends.append(cp)
    mine = pltpu.make_async_copy(o_ref.at[c], out_ref.at[:, columns], own)
    mine.start()
    mine.wait()
    for cp in ends:
        cp.wait()


def give_back(o):
    dma = pltpu.SemaphoreType.DMA
    anywhere = pl.BlockSpec(memory_space=pl.ANY)
    return pl.pallas_call(
        return_kernel,
        out_shape=jax.ShapeDtypeStruct((BLK, 64 * HEAD_DIM), jnp.bfloat16),
        in_specs=[anywhere],
        out_specs=anywhere,
        scratch_shapes=[dma((15,)), dma((15,)), dma],
        compiler_params=pltpu.CompilerParams(collective_id=1, has_side_effects=True),
    )(o)


def on_device(queries, keys, values, doc_lengths):
    q, kv = gather(queries, keys, values)
    o = attend(doc_lengths, q, kv)
    return give_back(o)


def solution(mesh):
    rows = P(("ctx", "head"), None)
    return jax.shard_map(on_device, mesh=mesh, in_specs=(rows, rows, rows, P()), out_specs=rows, check_vma=False)
```

time: 133 us -> 117 us (0.88)
  the two profiles are of different devices: /device:TPU:17 before, /device:TPU:1 now
where the time goes in v2:
time: 117 us
  Pallas kernels  114 us (97%)
  local copies, waits for them, and re-layouts  3.1 us (3%)
    pallas_call x1, Pallas kernels, gather(): pl.pallas_call(gather_kernel, out_shape=(jax.ShapeDtypeStruct((NB, BLK, Q...  52.5 us
    pallas_call x1, Pallas kernels, attend(): pl.pallas_call(attend_kernel, out_shape=jax.ShapeDtypeStruct((NB, BLK, QW...  32.9 us
    pallas_call x1, Pallas kernels, give_back(): pl.pallas_call(return_kernel, out_shape=jax.ShapeDtypeStruct((BLK, 64 * H...  28.3 us
    unnamed x1, local copies, waits for them, and re-layouts  3.1 us

profile of v2, /device:TPU:1, one launch (start us, length us, event | category | flops | bytes accessed | tf_op | source)
XLA Modules:
  0.0 116.8 jit_solution(18096559090745862773)
XLA Ops:
  0.0 52.5 %shard_map.46 = (bf16[16,128,512]{2,1,0:T(8,128)(2,1)}, bf16[2,16,8,128,128]{4,3,2,1,0:T(8,128)(2,1)}) custom-call(bf16[128,8192]{1,0:T(8,128)(2,1)} %q_ref.1, bf16[128,1024]{1,0:T(8,128)(2,1)} %k_ref.1, bf16[128,1024]{1,0:T(8,128)(2,1)} %v_ref.1), custom_call_target="tpu_custom_call" | custom-call | tf_op jit(solution)/shard_map/pallas_call | solution.py:159
  52.5 32.9 %shard_map.47.o_ref = bf16[16,128,512]{2,1,0:T(8,128)(2,1)} custom-call(s32[8]{0:T(128)} %lengths.1, bf16[16,128,512]{2,1,0:T(8,128)(2,1)} %get-tuple-element.7.q_hbm, bf16[2,16,8,128,128]{4,3,2,1,0:T(8,128)(2,1)} %get-tuple-element.8.kv_ref), custom_call_target="tpu_custom_call" | custom-call | tf_op jit(solution)/shard_map/pallas_call | solution.py:326
  85.4 28.3 %shard_map.48 = bf16[128,8192]{1,0:T(8,128)(2,1)} custom-call(bf16[16,128,512]{2,1,0:T(8,128)(2,1)} %shard_map.47.o_ref), custom_call_target="tpu_custom_call" | custom-call | tf_op jit(solution)/shard_map/pallas_call | solution.py:383
  113.7 3.1 %copy.6 = bf16[128,8192]{1,0:T(8,128)(2,1)} copy(bf16[128,8192]{1,0:T(8,128)(2,1)} %shard_map.48) | data formatting | bytes 4194304

commit v3 on v2

--- a/solution.py
+++ b/solution.py
@@ -15,7 +15,8 @@
 SPAN = 1024
 QW = 512
 KT = 512
-DIAG = 4
+NEAR = 7 * 128
+UNROLL = 1
 SCALE2 = HEAD_DIM ** -0.5 * 1.4426950408889634
 NEG = -1e30
 
@@ -173,7 +174,7 @@
 
 
 def attend_kernel(
-    lengths, q_hbm, kv_ref, o_hbm, q_ref, o_ref, kd, vd, kb, vb, ka, qa, m_ref, a_ref, lo_ref, next_ref,
+    lengths, q_hbm, kv_ref, m_hbm, a_hbm, q_ref, kb, vb, ka, qa, m_ref, a_ref, lo_ref, next_ref,
     s0, s1, p0, p1, f0, f1, x0, x1, load, store,
 ):
     sb, pb, fb, xb = (s0, s1), (p0, p1), (f0, f1), (x0, x1)
@@ -181,10 +182,8 @@
     bf = jnp.bfloat16
     copies = [
         pltpu.make_async_copy(q_hbm, q_ref, load.at[0]),
-        pltpu.make_async_copy(kv_ref.at[0, :, j], kd, load.at[1]),
-        pltpu.make_async_copy(kv_ref.at[1, :, j], vd, load.at[2]),
-        pltpu.make_async_copy(kv_ref.at[0], kb.at[pl.ds(1, NB)], load.at[3]),
-        pltpu.make_async_copy(kv_ref.at[1], vb.at[pl.ds(1, NB)], load.at[4]),
+        pltpu.make_async_copy(kv_ref.at[0], kb.at[pl.ds(1, NB)], load.at[1]),
+        pltpu.make_async_copy(kv_ref.at[1], vb.at[pl.ds(1, NB)], load.at[2]),
     ]
     for cp in copies:
         cp.start()
@@ -217,11 +216,13 @@
         for d in range(NDOCS - 1):
             low = jnp.where(p >= ends[d], ends[d], low)
         lo_ref[i] = low
-        total = total + (p - low + KT - 1) // KT
+        total = total + jnp.maximum(p - NEAR - low + KT - 1, 0) // KT
     follow = jnp.int32(NB - 1)
     for i in range(NB - 1, -1, -1):
         next_ref[i] = follow
-        follow = jnp.where(i * SPAN + j * BLK > lo_ref[i], i, follow)
+        follow = jnp.where(i * SPAN + j * BLK - NEAR > lo_ref[i], i, follow)
+    m_ref[...] = jnp.full(m_ref.shape, NEG, jnp.float32)
+    a_ref[...] = jnp.zeros(a_ref.shape, jnp.float32)
     p1[...] = jnp.zeros(p1.shape, bf)
     f1[...] = jnp.ones(f1.shape, jnp.float32)
 
@@ -237,29 +238,8 @@
     def with_ones(vt):
         return jnp.concatenate([vt, jnp.ones((16, vt.shape[1]), bf)], 0)
 
-    for cp in copies[:3]:
+    for cp in copies:
         cp.wait()
-    below = place <= lax.broadcasted_iota(jnp.int32, (BLK, BLK), 1)
-
-    def diagonal(g, _):
-        blocks = [g * DIAG + u for u in range(DIAG)]
-        scores = []
-        for b in blocks:
-            s = product(jnp.concatenate([kd[b], ka[b + 1, j]], 1), queries(b))
-            scores.append(jnp.concatenate([jnp.where(below, s[:, h * 128 : (h + 1) * 128], NEG) for h in range(4)], 1))
-        parts = []
-        for b, s in zip(blocks, scores):
-            top = jnp.max(s, axis=0, keepdims=True)
-            m_ref[b] = top
-            parts.append(jnp.exp2((s - top) * SCALE2).astype(bf))
-        for b, p in zip(blocks, parts):
-            a_ref[b] = jnp.dot(with_ones(vd[b]), p, preferred_element_type=jnp.float32)
-        return 0
-
-    lax.fori_loop(0, NB // DIAG, diagonal, 0)
-    for cp in copies[3:]:
-        cp.wait()
-
     kf, af, vf = (r.reshape((NB + 1) * 8, BLK, HEAD_DIM) for r in (kb, ka, vb))
     steps = KT // BLK
 
@@ -268,7 +248,7 @@
         done = low <= lo_ref[b]
         b_new = jnp.where(done, next_ref[b], b)
         over = (done & (b_new <= b)) | (top <= 0)
-        return b_new, jnp.where(over, 0, jnp.where(done, b_new * SPAN + j * BLK, low))
+        return b_new, jnp.where(over, 0, jnp.where(done, b_new * SPAN + j * BLK - NEAR, low))
 
     def window(top):
         return (jnp.maximum(top, 0) - KT + SPAN) // BLK
@@ -292,7 +272,7 @@
         vt = jnp.concatenate([vf[at + t] for t in range(steps)], 1)
         a_ref[b] = a_ref[b] * f_ref[...] + jnp.dot(with_ones(vt), p_ref[...], preferred_element_type=jnp.float32)
 
-    b0, top0 = follow, follow * SPAN + j * BLK
+    b0, top0 = follow, follow * SPAN + j * BLK - NEAR
     score(b0, top0, sb[0], xb[0])
 
     def body(_, carry):
@@ -308,16 +288,11 @@
 
     lax.fori_loop(0, jnp.where(total > 0, (total + 4) // 4, 0), body, (b0, top0, b0, top0))
 
-    def finish(i, _):
-        out = a_ref[i, 0:128] * (1.0 / a_ref[i, 128:129])
-        for h in range(4):
-            o_ref[i, :, h * 128 : (h + 1) * 128] = out[:, h * 128 : (h + 1) * 128].T.astype(bf)
-        pltpu.make_async_copy(o_ref.at[i], o_hbm.at[i], store.at[i]).start()
-        return 0
-
-    lax.fori_loop(0, NB, finish, 0)
-    for i in range(NB):
-        pltpu.make_async_copy(o_ref.at[i], o_hbm.at[i], store.at[i]).wait()
+    out = [pltpu.make_async_copy(m_ref, m_hbm, store.at[0]), pltpu.make_async_copy(a_ref, a_hbm, store.at[1])]
+    for cp in out:
+        cp.start()
+    for cp in out:
+        cp.wait()
 
 
 def attend(lengths, q, kv):
@@ -325,17 +300,14 @@
     anywhere = pl.BlockSpec(memory_space=pl.ANY)
     return pl.pallas_call(
         attend_kernel,
-        out_shape=jax.ShapeDtypeStruct((NB, BLK, QW), bf),
+        out_shape=(jax.ShapeDtypeStruct((NB, 1, QW), f32), jax.ShapeDtypeStruct((NB, 144, QW), f32)),
         grid_spec=pltpu.PrefetchScalarGridSpec(
             num_scalar_prefetch=1,
             grid=(),
             in_specs=[anywhere] * 2,
-            out_specs=anywhere,
+            out_specs=(anywhere, anywhere),
             scratch_shapes=[
                 vmem((NB, BLK, QW), bf),
-                vmem((NB, BLK, QW), bf),
-                vmem((NB, BLK, HEAD_DIM), bf),
-                vmem((NB, HEAD_DIM, BLK), bf),
                 vmem((NB + 1, 8, BLK, HEAD_DIM), bf),
                 vmem((NB + 1, 8, HEAD_DIM, BLK), bf),
                 vmem((NB + 1, 8, BLK, BLK), bf),
@@ -352,48 +324,136 @@
                 vmem((1, QW), f32),
                 vmem((1, QW), f32),
                 vmem((1, QW), f32),
-                pltpu.SemaphoreType.DMA((5,)),
-                pltpu.SemaphoreType.DMA((NB,)),
+                pltpu.SemaphoreType.DMA((3,)),
+                pltpu.SemaphoreType.DMA((2,)),
             ],
         ),
         compiler_params=pltpu.CompilerParams(vmem_limit_bytes=56 * 2**20),
     )(lengths, q, kv)
 
 
-def return_kernel(o_ref, out_ref, send, recv, own):
+def return_kernel(
+    lengths, q_hbm, kv_hbm, m_hbm, a_hbm, out_ref, q_ref, k_ref, v_ref, m_ref, a_ref, o_ref, load, load_m, send, recv, own
+):
     c, j = lax.axis_index("ctx"), lax.axis_index("head")
-    others = ctx_peers(c)
-    enter([{"ctx": o, "head": j} for o in others])
-    columns = pl.ds(pl.multiple_of(kv_head(c, j) * 1024 + lax.rem(c, 2) * QW, QW), QW)
-    ends = []
-    for n, o in enumerate(others):
-        cp = remote(o_ref.at[o], out_ref.at[:, columns], send.at[n], recv.at[n], {"ctx": o, "head": j})
-        cp.start()
-        ends.append(cp)
-    mine = pltpu.make_async_copy(o_ref.at[c], out_ref.at[:, columns], own)
+    core, z, y = lax.rem(c, 2), lax.rem(c // 2, 4), c // 8
+    bf = jnp.bfloat16
+
+    def place(t):
+        q = t // 4
+        return (
+            lax.rem(y + 1 - q // 2, 2) * 8
+            + lax.rem(z + 3 - lax.rem(t, 4), 4) * 2
+            + lax.rem(core + lax.rem((q + 1) // 2, 2), 2)
+        )
+
+    def oldest(i):
+        return i * 8 + (j - 7) * ((i + 15) // 16)
+
+    def loads(t):
+        i = place(t)
+        keys = pl.ds(oldest(i), 8)
+        return [
+            pltpu.make_async_copy(q_hbm.at[i], q_ref.at[t], load.at[0, t]),
+            pltpu.make_async_copy(kv_hbm.at[0, keys], k_ref.at[t], load.at[1, t]),
+            pltpu.make_async_copy(kv_hbm.at[1, keys], v_ref.at[t], load.at[2, t]),
+            pltpu.make_async_copy(a_hbm.at[i], a_ref.at[t], load.at[3, t]),
+        ]
+
+    states = pltpu.make_async_copy(m_hbm, m_ref, load_m)
+    states.start()
+    for t in range(4):
+        for cp in loads(t):
+            cp.start()
+    barrier = pltpu.get_barrier_semaphore()
+    for t in range(NB - 1):
+        pl.semaphore_signal(barrier, inc=1, device_id={"ctx": place(t), "head": j}, device_id_type=MESH)
+    for t in range(4, NB):
+        for cp in loads(t):
+            cp.start()
+    pl.semaphore_wait(barrier, NB - 1)
+    states.wait()
+    columns = pl.ds(pl.multiple_of(kv_head(c, j) * 1024 + core * QW, QW), QW)
+    lane = lax.broadcasted_iota(jnp.int32, (1, BLK), 1)
+    key = lax.broadcasted_iota(jnp.int32, (SPAN, BLK), 0)
+
+    def returned(t):
+        return remote(o_ref.at[t], out_ref.at[:, columns], send.at[t], recv.at[t], {"ctx": place(t), "head": j})
+
+    def step(g, _):
+        turns = [g * UNROLL + u for u in range(UNROLL)]
+        for t in turns:
+            for cp in loads(t):
+                cp.wait()
+        scores, parts, factors = [], [], []
+        for t in turns:
+            i = place(t)
+            q = jnp.concatenate([q_ref[t, :, h * 128 : (h + 1) * 128] for h in range(4)], 0)
+            s = lax.dot_general(
+                k_ref[t].reshape(SPAN, HEAD_DIM), q, (((1,), (1,)), ((), ())), preferred_element_type=jnp.float32
+            )
+            row = lane + (i * SPAN + j * BLK)
+            start, end = jnp.zeros((1, BLK), jnp.int32), jnp.int32(0)
+            for d in range(NDOCS - 1):
+                end = end + lengths[d]
+                start = jnp.where(row >= end, end, start)
+            base = oldest(i) * BLK
+            seen = (key >= start - base) & (key <= row - base)
+            s = jnp.concatenate([jnp.where(seen, s[:, h * 128 : (h + 1) * 128], NEG) for h in range(4)], 1)
+            old = m_ref[i]
+            top = jnp.maximum(old, jnp.max(s, axis=0, keepdims=True))
+            factors.append(jnp.exp2((old - top) * SCALE2))
+            parts.append(jnp.exp2((s - top) * SCALE2).astype(bf))
+        for u, t in enumerate(turns):
+            vt = jnp.concatenate([v_ref[t, n] for n in range(8)], 1)
+            vt = jnp.concatenate([vt, jnp.ones((16, SPAN), bf)], 0)
+            a = a_ref[t] * factors[u] + jnp.dot(vt, parts[u], preferred_element_type=jnp.float32)
+            out = a[0:128] * (1.0 / a[128:129])
+            for h in range(4):
+                o_ref[t, :, h * 128 : (h + 1) * 128] = out[:, h * 128 : (h + 1) * 128].T.astype(bf)
+
+            @pl.when(t < NB - 1)
+            def _():
+                returned(t).start()
+
+        return 0
+
+    lax.fori_loop(0, NB // UNROLL, step, 0)
+    mine = pltpu.make_async_copy(o_ref.at[NB - 1], out_ref.at[:, columns], own)
     mine.start()
     mine.wait()
-    for cp in ends:
-        cp.wait()
-
-
-def give_back(o):
+    for t in range(NB - 1):
+        returned(t).wait()
+
+
+def give_back(lengths, q, kv, m, a):
+    f32, bf, vmem = jnp.float32, jnp.bfloat16, pltpu.VMEM
     dma = pltpu.SemaphoreType.DMA
     anywhere = pl.BlockSpec(memory_space=pl.ANY)
     return pl.pallas_call(
         return_kernel,
-        out_shape=jax.ShapeDtypeStruct((BLK, 64 * HEAD_DIM), jnp.bfloat16),
-        in_specs=[anywhere],
+        out_shape=jax.ShapeDtypeStruct((BLK, 64 * HEAD_DIM), bf),
+        in_specs=[pl.BlockSpec(memory_space=pltpu.SMEM)] + [anywhere] * 4,
         out_specs=anywhere,
-        scratch_shapes=[dma((15,)), dma((15,)), dma],
-        compiler_params=pltpu.CompilerParams(collective_id=1, has_side_effects=True),
-    )(o)
+        scratch_shapes=[
+            vmem((NB, BLK, QW), bf),
+            vmem((NB, 8, BLK, HEAD_DIM), bf),
+            vmem((NB, 8, HEAD_DIM, BLK), bf),
+            vmem((NB, 1, QW), f32),
+            vmem((NB, 144, QW), f32),
+            vmem((NB, BLK, QW), bf),
+            dma((4, NB)), dma, dma((NB,)), dma((NB,)), dma,
+        ],
+        compiler_params=pltpu.CompilerParams(
+            collective_id=1, has_side_effects=True, vmem_limit_bytes=56 * 2**20
+        ),
+    )(lengths, q, kv, m, a)
 
 
 def on_device(queries, keys, values, doc_lengths):
     q, kv = gather(queries, keys, values)
-    o = attend(doc_lengths, q, kv)
-    return give_back(o)
+    m, a = attend(doc_lengths, q, kv)
+    return give_back(doc_lengths, q, kv.reshape(2, NB * 8, BLK, HEAD_DIM), m, a)
 
 
 def solution(mesh):

time: 117 us -> 115 us (0.983)
  the two profiles are of different devices: /device:TPU:1 before, /device:TPU:17 now
where the time goes in v3:
time: 115 us; the launch traced here: 113 us
  Pallas kernels  110 us (96%)
  local copies, waits for them, and re-layouts  3.1 us (3%)
    pallas_call x1, Pallas kernels, gather(): pl.pallas_call(gather_kernel, out_shape=(jax.ShapeDtypeStruct((NB, BLK, Q...  49.3 us
    pallas_call x1, Pallas kernels, give_back(): pl.pallas_call(return_kernel, out_shape=jax.ShapeDtypeStruct((BLK, 64 * H...  36.3 us
    pallas_call x1, Pallas kernels, attend(): pl.pallas_call(attend_kernel, out_shape=(jax.ShapeDtypeStruct((NB, 1, QW)...  24.1 us
    unnamed x1, local copies, waits for them, and re-layouts  3.1 us

profile of v3, /device:TPU:17, one launch (start us, length us, event | category | flops | bytes accessed | tf_op | source)
XLA Modules:
  0.0 112.8 jit_solution(2810345617992274711)
XLA Ops:
  0.0 49.3 %shard_map.46 = (bf16[16,128,512]{2,1,0:T(8,128)(2,1)}, bf16[2,16,8,128,128]{4,3,2,1,0:T(8,128)(2,1)}) custom-call(bf16[128,8192]{1,0:T(8,128)(2,1)} %q_ref.1, bf16[128,1024]{1,0:T(8,128)(2,1)} %k_ref.1, bf16[128,1024]{1,0:T(8,128)(2,1)} %v_ref.1), custom_call_target="tpu_custom_call" | custom-call | tf_op jit(solution)/shard_map/pallas_call | solution.py:160
  49.3 24.1 %shard_map.47 = (f32[16,1,512]{2,1,0:T(1,128)}, f32[16,144,512]{2,1,0:T(8,128)}) custom-call(s32[8]{0:T(128)} %lengths.3, bf16[16,128,512]{2,1,0:T(8,128)(2,1)} %get-tuple-element.9.q_hbm, bf16[2,16,8,128,128]{4,3,2,1,0:T(8,128)(2,1)} %get-tuple-element.10.kv_ref), custom_call_target="tpu_custom_call" | custom-call | tf_op jit(solution)/shard_map/pallas_call | solution.py:301
  73.4 36.3 %shard_map.48 = bf16[128,8192]{1,0:T(8,128)(2,1)} custom-call(s32[8]{0:T(128)} %lengths.3, bf16[16,128,512]{2,1,0:T(8,128)(2,1)} %get-tuple-element.9.q_hbm, bf16[2,128,128,128]{3,2,1,0:T(8,128)(2,1)} %bitcast.1, f32[16,1,512]{2,1,0:T(1,128)} %get-tuple-element.11.m_hbm, f32[16,144,512]{2,1,0:T(8,128)} %get-tuple-element.12.a_hbm), custom_call_target="tpu_custom_call" | custom-call | tf_op jit(solution)/shard_map/pallas_call | solution.py:433
  109.7 3.1 %copy.6 = bf16[128,8192]{1,0:T(8,128)(2,1)} copy(bf16[128,8192]{1,0:T(8,128)(2,1)} %shard_map.48) | data formatting | bytes 4194304
